TPU v7x, 32 devices: a whole 2x2x4 slice. The times are simulated.
32 devices in a mesh: groups: 2 (over y), tile: 4 (over z), segment: 2 (over core), mp: 2 (over x).
Axes of the slice: x: 2, y: 2, z: 4, core: 2. Of those that a mesh axis runs over, the one named last changes fastest.
Arguments:
- spectra: bfloat16 [2, 64, 48, 224], P(None, ('groups', 'tile')), parts along dimension 1, may hold values from -6 to 6
- valid: int32 [2, 64], P(None, 'groups'), parts along dimension 1, may hold values from 1 to 48, as said below
- project: bfloat16 [224, 16], replicated, may hold values from -0.375 to 0.375
- enc_in: bfloat16 [768, 3072], P(None, 'mp'), may hold values from -0.21875 to 0.21875
- enc_out: bfloat16 [3072, 768], P('mp'), may hold values from -0.109375 to 0.109375
- tok_embed: bfloat16 [48, 2048], replicated, may hold values from -0.875 to 0.875
- band_embed: bfloat16 [16, 2048], P('tile'), may hold values from -3 to 3
- dec_in: bfloat16 [2048, 8192], P('tile', 'mp'), may hold values from -0.125 to 0.125
- dec_out: bfloat16 [8192, 2048], P('mp', 'tile'), may hold values from -0.0625 to 0.0625
- head: bfloat16 [2048, 672], P('tile', 'mp'), may hold values from -0.125 to 0.125
Outputs:
- grad_project: float32 [448, 16], P(('groups', 'tile', 'segment')), parts along dimension 0
- grad_enc_in: float32 [1536, 3072], P(('groups', 'tile', 'segment'), 'mp'), parts along dimension 0
- grad_enc_out: float32 [6144, 768], P(('groups', 'mp'), ('tile', 'segment')), parts along dimension 0
There are 2 independent parts, one for each index of `groups`. A program takes and returns all parts, laid end to end along the dimension named above; an argument that names none is the same for every part. Nothing has to cross between parts.
Inputs may be any that keep to these rules, and one draw needn't show every extreme that they name: Pixels of patch n in micro-batch m with index below valid[m, n] count in the loss.
All inputs are finite; a program needn't handle non-finite values.
Results may differ from a plain program's by a relative error of at most 0.018.
Values may be sent and summed in bfloat16 or wider, within the bound.
A program may use at most 128 MiB of HBM per device.

v0:
```python
import jax
import jax.numpy as jnp
from jax import lax
from jax.sharding import PartitionSpec as P

BF = jnp.bfloat16
F32 = jnp.float32


def inv_rms(values):
    return lax.rsqrt(jnp.mean(values * values, axis=-1, keepdims=True) + 1e-05)


def rms_back(values, gradient):
    scaling = inv_rms(values)
    normed = values * scaling
    return scaling * (gradient - normed * jnp.mean(gradient * normed, axis=-1, keepdims=True))


def gelu(v):
    return 0.5 * v * (1 + jnp.tanh(0.7978845608028654 * (v + 0.044715 * v * v * v)))


def gelu_and_slope(v):
    square = v * v
    t = jnp.tanh(0.7978845608028654 * v * (1 + 0.044715 * square))
    half = 0.5 * (1 + t)
    slope = half + 0.5 * v * (1 - t * t) * 0.7978845608028654 * (1 + 3 * 0.044715 * square)
    return (v * half, slope)


def dot(a, b):
    return jnp.dot(a, b, preferred_element_type=F32)


def dot_t(a, b):
    return lax.dot_general(a, b, (((1,), (1,)), ((), ())), preferred_element_type=F32)


def t_dot(a, b):
    return lax.dot_general(a, b, (((0,), (0,)), ((), ())), preferred_element_type=F32)


def body(spectra, valid, project, enc_in, enc_out, tok_embed, band_embed, dec_in, dec_out, head):
    tile, seg, mp = (lax.axis_index(a) for a in ("tile", "segment", "mp"))
    T, S, M = (lax.axis_size(a) for a in ("tile", "segment", "mp"))
    batches, per_tile, pixels, bands = spectra.shape
    codes = project.shape[1]
    width = bands // codes
    local = batches * per_tile
    share = local // (S * M)
    rows = T * local
    student = codes * pixels
    dim = tok_embed.shape[1]
    dt = dec_in.shape[0]
    hid = dec_in.shape[1] // S
    once = jnp.logical_and(seg == 0, mp == 0).astype(F32)
    patches = spectra.reshape(local, pixels, bands)
    flat = patches.reshape(local * pixels, bands)
    feat_local = (
        dot(flat, project)
        .astype(BF)
        .reshape(local, pixels, codes)
        .transpose(0, 2, 1)
        .reshape(local, student)
    )
    feats = lax.all_gather(feat_local, "tile")
    feats = feats.reshape(T, S, M, share, student).transpose(1, 2, 0, 3, 4).reshape(rows, student)
    band_all = lax.all_gather(band_embed, "tile", tiled=True)
    head_full = lax.all_gather(head, "mp", axis=1, tiled=True)
    embed = jnp.concatenate([tok_embed, band_all], axis=0)
    embed_z = lax.dynamic_slice_in_dim(embed, tile * dt, dt, 1)
    d_in = lax.dynamic_slice_in_dim(dec_in, seg * hid, hid, 1)
    d_out = lax.dynamic_slice_in_dim(dec_out, seg * hid, hid, 0)
    folded = lax.psum(dot(embed_z, d_in).astype(BF), "tile")
    fold_tok, fold_band = (folded[:pixels], folded[pixels:])
    feats32 = feats.astype(F32)
    normed = (feats32 * inv_rms(feats32)).astype(BF)
    pre_act, pre_slope = gelu_and_slope(dot(normed, enc_in))
    act_out = pre_act.astype(BF)
    summed = lax.psum(dot(act_out, enc_out).astype(BF), "mp").astype(F32)
    encoded = (feats32 + summed).astype(BF)
    tokens = rows * codes
    tok = encoded.reshape(tokens, pixels)
    embedded = (
        (dot(tok, tok_embed).reshape(rows, codes, dim) + band_all.astype(F32))
        .reshape(tokens, dim)
        .astype(BF)
    )
    scaling = inv_rms(embedded.astype(F32))
    hid_pre = scaling * (
        dot(tok, fold_tok).reshape(rows, codes, hid) + fold_band.astype(F32)
    ).reshape(tokens, hid)
    hid_act, hid_slope = gelu_and_slope(hid_pre)
    embedded_z = lax.dynamic_slice_in_dim(embedded, tile * dt, dt, 1)
    decoded = (once * embedded_z.astype(F32) + dot(hid_act.astype(BF), d_out)).astype(BF)
    partial = dot(decoded, head_full).astype(BF)
    own = lax.psum_scatter(
        partial.reshape(S * M, T, share * codes, -1), ("segment", "mp"), scatter_dimension=0
    )
    own = lax.psum_scatter(own, "tile", scatter_dimension=0).astype(F32)
    quarter = (seg * M + mp) * share
    own_patches = lax.dynamic_slice_in_dim(patches, quarter, share, 0)
    target = (
        own_patches.reshape(share, pixels, codes, width)
        .transpose(0, 2, 1, 3)
        .reshape(share * codes, -1)
    )
    total_valid = jnp.sum(valid.astype(F32))
    loss_scale = 2.0 * batches * valid.shape[1] / total_valid
    own_valid = lax.dynamic_slice_in_dim(valid, tile * per_tile, per_tile, 1).reshape(local)
    own_valid = lax.dynamic_slice_in_dim(own_valid, quarter, share, 0)
    column = jnp.arange(pixels * width, dtype=jnp.int32) // width
    mask = (column[None, :] < jnp.repeat(own_valid, codes)[:, None]).astype(F32)
    grad_own = (loss_scale * mask * (own - target.astype(F32))).astype(BF)
    grad_rebuilt = lax.all_gather(lax.all_gather(grad_own, "tile"), ("segment", "mp")).reshape(
        tokens, -1
    )
    grad_decoded = dot_t(grad_rebuilt, head_full).astype(BF)
    grad_hid = hid_slope * dot_t(grad_decoded, d_out)
    tok_z = lax.dynamic_slice_in_dim(tok_embed, tile * dt, dt, 1)
    unit_tok = dot_t((embedded.astype(F32) * scaling).astype(BF), tok_embed)
    along = jnp.sum(grad_hid * hid_pre, axis=1, keepdims=True) / dim
    grad_tok = scaling * (dot_t(grad_hid.astype(BF), fold_tok) - unit_tok * along)
    grad_tok = grad_tok + once * dot_t(grad_decoded, tok_z)
    grad_encoded = lax.psum(grad_tok.reshape(rows, student).astype(BF), ("tile", "segment", "mp"))
    grad_act = (pre_slope * dot_t(grad_encoded, enc_out)).astype(BF)
    columns = student // (T * S)
    start = (tile * S + seg) * columns
    grad_out = t_dot(act_out, lax.dynamic_slice_in_dim(grad_encoded, start, columns, 1))
    grad_in = t_dot(lax.dynamic_slice_in_dim(normed, start, columns, 1), grad_act)
    grad_normed = lax.psum(dot_t(grad_act, enc_in).astype(BF), "mp").astype(F32)
    own_rows = lambda a: lax.dynamic_slice_in_dim(
        a.reshape(S * M, T, share, student), tile, 1, 1
    ).reshape(local, student)
    grad_feat = (
        own_rows(grad_encoded).astype(F32) + rms_back(feat_local.astype(F32), own_rows(grad_normed))
    ).astype(BF)
    grad_codes = grad_feat.reshape(local, codes, pixels).transpose(0, 2, 1).reshape(-1, codes)
    grad_proj = jnp.sum(lax.all_gather(t_dot(flat, grad_codes), "tile"), axis=0)
    proj_rows = bands // (T * S)
    grad_proj = lax.dynamic_slice_in_dim(grad_proj, (tile * S + seg) * proj_rows, proj_rows, 0)
    return (grad_proj, grad_in, grad_out)


def solution(mesh):
    placed = (
        P(None, ("groups", "tile"), None, None),
        P(None, "groups"),
        P(),
        P(None, "mp"),
        P("mp", None),
        P(),
        P("tile", None),
        P("tile", "mp"),
        P("mp", "tile"),
        P("tile", "mp"),
    )
    return jax.shard_map(
        body,
        mesh=mesh,
        in_specs=placed,
        out_specs=(
            P(("groups", "tile", "segment"), None),
            P(("groups", "tile", "segment"), "mp"),
            P(("groups", "mp"), ("tile", "segment")),
        ),
        check_vma=False,
    )
```

profile of v0, /device:TPU:0, one launch (start us, length us, event | category | flops | bytes accessed | tf_op | source)
XLA Modules:
  0.0 350.5 jit_solution(10092934858017082224)
XLA Ops:
  7.2 1.4 convolution_convert_fusion.5
  8.8 0.7 fusion.49
  9.6 15.0 %all_gather.25 = bf16[4,16,768]{2,1,0:T(8,128)(2,1)S(1)} all-gather(bf16[1,16,768]{2,1,0:T(8,128)(2,1)S(1)} %all_gather_reshape.3), channel_id=1, replica_groups=mesh['groups'=2,'tile'=4,'segment'=2,'mp'=2] {'tile'}, dimensions={0}, use_global_device_ids=true | all-gather | bytes 122880 | tf_op jit(solution)/shard_map/all_gather | solution.py:67
  25.2 2.2 fusion.50
  27.4 0.7 copy-done.3
  28.2 1.2 convolution_convert_fusion.4
  29.5 13.3 %all-gather.2 = bf16[4,4,2048]{2,1,0:T(4,128)(2,1)S(1)} all-gather(bf16[1,4,2048]{2,1,0:T(4,128)(2,1)S(1)} %bitcast.88), channel_id=1, replica_groups=mesh['groups'=2,'tile'=4,'segment'=2,'mp'=2] {'tile'}, dimensions={0}, use_global_device_ids=true | all-gather | bytes 81920 | tf_op jit(solution)/shard_map/all_gather | solution.py:69
  42.8 2.8 convolution_convert_fusion
  45.7 0.7 convert_element_type.165
  46.4 8.4 %all_gather.27 = bf16[512,672]{0,1:T(8,128)(2,1)S(1)} all-gather(bf16[512,336]{0,1:T(8,128)(2,1)} %param.19), channel_id=1, replica_groups=mesh['groups'=2,'tile'=4,'segment'=2,'mp'=2] {'mp'}, dimensions={1}, use_global_device_ids=true | all-gather | bytes 1032192 | tf_op jit(solution)/shard_map/all_gather | solution.py:70
  54.7 1.0 add_convert_fusion.2
  55.8 0.3 dot_general.61
  56.1 4.2 %multiply_reduce_fusion.1 = (f32[64,16]{1,0:T(8,128)S(1)}, bf16[64,16,2048]{2,1,0:T(8,128)(2,1)}) fusion(f32[16,2048]{1,0:T(8,128)} %convert_element_type.165, bf16[64,16,48]{2,1,0:T(8,128)(2,1)S(1)} %dot_general.61, bf16[48,2048]{1,0:T(8,128)(2,1)} %param.15), kind=kOutput, calls=%fused_computation.7 | convolution fusion | flops 211811328 | bytes 4624384 | tf_op jit(solution)/shard_map/dot_general | solution.py:33
  60.4 29.6 %all-reduce.7.cloned.1.call-done = bf16[64,2048]{1,0:T(8,128)(2,1)} async-done(((bf16[64,2048]{1,0:T(8,128)(2,1)}), bf16[64,2048]{1,0:T(8,128)(2,1)}) %all-reduce.7.cloned.1.call-update) | async-done | bytes 262160 | tf_op jit(solution)/shard_map/psum | solution.py:75
  90.0 0.8 slice_convert_fusion
  90.8 2.2 convolution_add_fusion
  93.0 5.3 %multiply_convert_fusion.1 = bf16[1024,2048]{1,0:T(8,128)(2,1)} fusion(f32[64,16,2048]{2,1,0:T(8,128)S(1)} %convolution_add_fusion, f32[1024]{0:T(1024)S(1)} %rsqrt.37), kind=kLoop, calls=%fused_computation.3 | loop fusion | flops 20971520 | bytes 12587008 | tf_op jit(solution)/shard_map/convert_element_type | solution.py:96
  98.3 7.2 %convolution_convert_fusion.1 = bf16[1024,672]{0,1:T(8,128)(2,1)} fusion(bf16[512,672]{0,1:T(8,128)(2,1)S(1)} %all_gather.27, bf16[1024,2048]{1,0:T(8,128)(2,1)} %multiply_convert_fusion.1, bf16[4096,512]{1,0:T(8,128)(2,1)} %param.18, s32[]{:T(128)S(6)} %select_n.37, bf16[1024,2048]{1,0:T(8,128)(2,1)} %bitcast.90, s32[]{:T(128)S(6)} %select_n.36, ...), kind=kOutput, calls=%fused_computation.22 | convolution fusion | flops 2854912000 | bytes 9404428 | tf_op jit(solution)/shard_map/dot_general | solution.py:33
  105.5 2.6 copy.40
  108.2 28.0 %reduce-scatter.3.cloned.1.call-done = bf16[1,4,64,672]{3,2,1,0:T(8,128)(2,1)} async-done(((bf16[4,4,64,672]{3,2,1,0:T(8,128)(2,1)}), bf16[1,4,64,672]{3,2,1,0:T(8,128)(2,1)}) %reduce-scatter.3.cloned.1.call-update) | async-done | bytes 344080 | tf_op jit(solution)/shard_map/reduce_scatter | solution.py:98
  136.9 1.8 copy.42
  138.7 1.9 reshape.268
  140.7 0.6 convert_reduce_fusion
  142.0 17.0 %reduce-scatter.5.cloned.1.call-done = bf16[1,64,672]{2,1,0:T(8,128)(2,1)} async-done(((bf16[4,64,672]{2,1,0:T(8,128)(2,1)}), bf16[1,64,672]{2,1,0:T(8,128)(2,1)}) %reduce-scatter.5.cloned.1.call-update) | async-done | bytes 86032 | tf_op jit(solution)/shard_map/reduce_scatter | solution.py:101
  159.0 1.0 multiply_convert_fusion.6
  160.0 15.8 %all_gather.28 = bf16[4,64,672]{2,1,0:T(8,128)(2,1)} all-gather(bf16[1,64,672]{2,1,0:T(8,128)(2,1)S(1)} %multiply_convert_fusion.6), channel_id=1, replica_groups=mesh['groups'=2,'tile'=4,'segment'=2,'mp'=2] {'tile'}, dimensions={0}, use_global_device_ids=true | all-gather | bytes 430080 | tf_op jit(solution)/shard_map/all_gather | solution.py:116
  176.2 17.2 %all-gather.6.cloned.1.call-done = bf16[16,64,672]{2,1,0:T(8,128)(2,1)} async-done(((bf16[4,64,672]{2,1,0:T(8,128)(2,1)}), bf16[16,64,672]{2,1,0:T(8,128)(2,1)}) %all-gather.6.cloned.1.call-update) | async-done | bytes 1376272 | tf_op jit(solution)/shard_map/all_gather | solution.py:116
  193.4 2.7 convolution_convert_fusion.2
  196.3 9.2 %multiply_reduce_fusion = (f32[1024]{0:T(1024)S(1)}, bf16[1024,2048]{1,0:T(8,128)(2,1)S(1)}) fusion(f32[64,16,2048]{2,1,0:T(8,128)} %copy-done.1, f32[1024]{0:T(1024)S(1)} %rsqrt.37, bf16[1024,512]{1,0:T(8,128)(2,1)S(1)} %convolution_convert_fusion.2, bf16[4096,512]{1,0:T(8,128)(2,1)S(1)} %copy-done.12, s32[]{:T(128)S(6)} %select_n.37), kind=kOutput, calls=%fused_computation.1 | convolution fusion | flops 2191522816 | bytes 15736836 | tf_op jit(solution)/shard_map/dot_general | solution.py:37
  205.5 0.4 convolution_multiply_fusion.1
  206.0 1.5 fusion.20
  207.5 2.0 fusion.21
  209.5 1.1 copy.43
  210.6 0.9 convert_element_type.188
  211.6 1.0 reshape.270
  212.7 86.1 %all-reduce.9.cloned.1.call-done = bf16[64,768]{1,0:T(8,128)(2,1)} async-done(((bf16[64,768]{1,0:T(8,128)(2,1)}), bf16[64,768]{1,0:T(8,128)(2,1)}) %all-reduce.9.cloned.1.call-update) | async-done | bytes 98320 | tf_op jit(solution)/shard_map/psum | solution.py:126
  298.8 1.7 fusion.4
  300.5 3.1 convolution_convert_fusion.3
  303.7 1.9 fusion.36
  305.6 0.9 reshape.261
  306.5 0.7 copy.45
  307.2 1.9 fusion.34
  309.1 0.9 reshape.260
  310.2 17.2 %all-reduce.11.cloned.1.call-done = bf16[4,4,4,768]{3,2,0,1:T(4,128)(2,1)} async-done(((bf16[4,4,4,768]{3,2,0,1:T(4,128)(2,1)}), bf16[4,4,4,768]{3,2,0,1:T(4,128)(2,1)}) %all-reduce.11.cloned.1.call-update) | async-done | bytes 98320 | tf_op jit(solution)/shard_map/psum | solution.py:132
  327.4 0.9 multiply_reduce_fusion.4
  328.4 0.7 dynamic-slice_convert_fusion.1
  329.7 13.3 %all-gather.3 = f32[4,224,16]{1,2,0:T(8,128)S(1)} all-gather(f32[1,224,16]{1,2,0:T(8,128)S(1)} %convolution_bitcast_fusion), channel_id=3, replica_groups=mesh['groups'=2,'tile'=4,'segment'=2,'mp'=2] {'tile'}, dimensions={0}, use_global_device_ids=true | all-gather | bytes 71680 | tf_op jit(solution)/shard_map/all_gather | solution.py:140
  342.9 0.7 constant_dynamic-slice_fusion
  (78 shorter events, 3.4 us)
Async XLA Ops:
  7.2 21.0 %copy-start = (bf16[1536,768]{1,0:T(8,128)(2,1)S(1)}, bf16[1536,768]{1,0:T(8,128)(2,1)}, u32[]{:S(2)}) copy-start(bf16[1536,768]{1,0:T(8,128)(2,1)} %param.14) | copy-start | bytes 7077892
  7.2 22.3 %copy-start.10 = (bf16[4,2048]{1,0:T(4,128)(2,1)S(1)}, bf16[4,2048]{1,0:T(4,128)(2,1)}, u32[]{:S(2)}) copy-start(bf16[4,2048]{1,0:T(4,128)(2,1)} %param.16) | copy-start | bytes 49156
  7.2 47.6 %all-reduce.5.cloned.1.call-start = ((), (), s32[]{:S(2)}) async-start(), calls=%async_computation.2 | async-start | bytes 196608 | tf_op jit(solution)/shard_map/psum | solution.py:81
  7.2 35.6 %copy-start.8 = (bf16[48,2048]{1,0:T(8,128)(2,1)S(1)}, bf16[48,2048]{1,0:T(8,128)(2,1)}, u32[]{:S(2)}) copy-start(bf16[48,2048]{1,0:T(8,128)(2,1)} %param.15) | copy-start | bytes 589828
  25.2 4.3 %copy-start.7 = (bf16[64,768]{1,0:T(8,128)(2,1)}, bf16[64,768]{1,0:T(8,128)(2,1)S(1)}, u32[]{:S(2)}) copy-start(bf16[64,768]{1,0:T(8,128)(2,1)S(1)} %multiply_convert_fusion.7) | copy-start | bytes 294916
  27.4 0.8 copy-start.3
  29.4 60.6 %all-reduce.7.cloned.1.call-start = ((), (), s32[]{:S(2)}) async-start(), calls=%async_computation.3 | async-start | bytes 524288 | tf_op jit(solution)/shard_map/psum | solution.py:75
  45.6 90.6 %reduce-scatter.3.cloned.1.call-start = ((), (), s32[]{:S(2)}) async-start(), calls=%async_computation.4 | async-start | bytes 1966080 | tf_op jit(solution)/shard_map/reduce_scatter | solution.py:98
  54.7 43.5 %copy-start.6 = (bf16[512,672]{0,1:T(8,128)(2,1)}, bf16[512,672]{0,1:T(8,128)(2,1)S(1)}, u32[]{:S(2)}) copy-start(bf16[512,672]{0,1:T(8,128)(2,1)S(1)} %all_gather.27) | copy-start | bytes 2064388
  93.0 5.3 %copy-start.1 = (f32[64,16,2048]{2,1,0:T(8,128)}, f32[64,16,2048]{2,1,0:T(8,128)S(1)}, u32[]{:S(2)}) copy-start(f32[64,16,2048]{2,1,0:T(8,128)S(1)} %convolution_add_fusion) | copy-start | bytes 25165828
  105.5 30.8 %copy-start.11 = (s32[2,32]{1,0:T(2,128)S(1)}, s32[2,32]{1,0:T(2,128)}, u32[]{:S(2)}) copy-start(s32[2,32]{1,0:T(2,128)} %param.11) | copy-start | bytes 772
  105.5 31.2 %copy-start.2 = (bf16[2,8,48,224]{3,2,1,0:T(8,128)(2,1)S(1)}, bf16[2,8,48,224]{3,2,1,0:T(8,128)(2,1)}, u32[]{:S(2)}) copy-start(bf16[2,8,48,224]{3,2,1,0:T(8,128)(2,1)} %param.10) | copy-start | bytes 1032196
  108.1 50.8 %reduce-scatter.5.cloned.1.call-start = ((), (), s32[]{:S(2)}) async-start(), calls=%async_computation.5 | async-start | bytes 491520 | tf_op jit(solution)/shard_map/reduce_scatter | solution.py:101
  136.2 57.2 %all-gather.6.cloned.1.call-start = ((), (), s32[]{:S(2)}) async-start(), calls=%async_computation.8 | async-start | bytes 1966080 | tf_op jit(solution)/shard_map/all_gather | solution.py:116
  175.8 123.0 %all-reduce.9.cloned.1.call-start = ((), (), s32[]{:S(2)}) async-start(), calls=%async_computation.6 | async-start | bytes 196608 | tf_op jit(solution)/shard_map/psum | solution.py:126
  193.4 2.9 copy-start.12
  196.3 9.2 %copy-start.9 = (bf16[48,2048]{1,0:T(8,128)(2,1)S(1)}, bf16[48,2048]{1,0:T(8,128)(2,1)}, u32[]{:S(2)}) copy-start(bf16[48,2048]{1,0:T(8,128)(2,1)} %param.15) | copy-start | bytes 589828
  196.3 9.7 %copy-start.13 = (bf16[64,16,2048]{2,1,0:T(8,128)(2,1)S(1)}, bf16[64,16,2048]{2,1,0:T(8,128)(2,1)}, u32[]{:S(2)}) copy-start(bf16[64,16,2048]{2,1,0:T(8,128)(2,1)} %get-tuple-element.6) | copy-start | bytes 12582916
  206.0 1.5 copy-start.5
  207.5 91.4 %copy-start.4 = (f32[64,1536]{1,0:T(8,128)S(1)}, f32[64,1536]{1,0:T(8,128)}, u32[]{:S(2)}) copy-start(f32[64,1536]{1,0:T(8,128)} %copy-done.3) | copy-start | bytes 1179652
  211.5 115.9 %all-reduce.11.cloned.1.call-start = ((), (), s32[]{:S(2)}) async-start(), calls=%async_computation.7 | async-start | bytes 196608 | tf_op jit(solution)/shard_map/psum | solution.py:132
Sparse Core Ops, SparseCore 0:
  29.5 22.1 all-reduce.4
  54.6 35.3 all-reduce.6
  108.3 27.9 reduce-scatter.2
  138.3 20.5 reduce-scatter.4
  175.9 17.4 all-gather.5
  211.6 87.1 all-reduce.8
  307.3 20.0 all-reduce.10
where the time goes:
time: 351 us; the launch traced here: 350 us
  waiting for transfers between devices  195 us (56%)
  blocking collectives  65.8 us (19%)
  matrix products  45.8 us (13%)
  local copies, waits for them, and re-layouts  15.7 us (4%)
  between operations  15.2 us (4%)
  other arithmetic  12.3 us (4%)
    psum x1, waiting for transfers between devices, body(): lax.psum(grad_tok.reshape(rows, student).astype(BF), ('tile', 'segment',...  86.1 us
    psum x1, waiting for transfers between devices, body(): folded = lax.psum(dot(embed_z, d_in).astype(BF), 'tile')  29.6 us
    reduce_scatter x1, waiting for transfers between devices, body(): lax.psum_scatter(partial.reshape(S * M, T, share * codes, -1), ('segment'...  28 us
    dot_general x7, matrix products, dot(): return jnp.dot(a, b, preferred_element_type=F32)  21.1 us
    dot_general x7, matrix products, dot_t(): lax.dot_general(a, b, (((1,), (1,)), ((), ())), preferred_element_type=F32)  20.7 us
    all_gather x1, waiting for transfers between devices, body(): lax.all_gather(lax.all_gather(grad_own, 'tile'), ('segment', 'mp'))  17.2 us
    psum x1, waiting for transfers between devices, body(): grad_normed = lax.psum(dot_t(grad_act, enc_in).astype(BF), 'mp').astype(F32)  17.2 us
    reduce_scatter x1, waiting for transfers between devices, body(): own = lax.psum_scatter(own, 'tile', scatter_dimension=0).astype(F32)  17 us
  transfers between devices with their start and end apart: 7, of which 6 were waited for; matrix products, arithmetic and copies ran while one was open for 5% of the time, Pallas kernels for 0%

commit v1 on v0

--- a/solution.py
+++ b/solution.py
@@ -123,7 +123,10 @@
     along = jnp.sum(grad_hid * hid_pre, axis=1, keepdims=True) / dim
     grad_tok = scaling * (dot_t(grad_hid.astype(BF), fold_tok) - unit_tok * along)
     grad_tok = grad_tok + once * dot_t(grad_decoded, tok_z)
-    grad_encoded = lax.psum(grad_tok.reshape(rows, student).astype(BF), ("tile", "segment", "mp"))
+    grad_encoded = jnp.sum(
+        lax.all_gather(grad_tok.reshape(rows, student).astype(BF), ("tile", "segment", "mp")),
+        axis=0,
+    )
     grad_act = (pre_slope * dot_t(grad_encoded, enc_out)).astype(BF)
     columns = student // (T * S)
     start = (tile * S + seg) * columns

time: 351 us -> 306 us (0.87)
  waiting for transfers between devices: 195 us -> 151 us
    psum x1 -> x0, waiting for transfers between devices: 86.1 us -> none  [body(): lax.psum(grad_tok.reshape(rows, student).astype(BF), ('tile', 'segment',...]
    all_gather x0 -> x1, waiting for transfers between devices: none -> 38.5 us  [body(): lax.all_gather(grad_tok.reshape(rows, student).astype(BF), ('tile', 'segm...]
where the time goes in v1:
time: 306 us
  waiting for transfers between devices  151 us (49%)
  blocking collectives  65.8 us (22%)
  matrix products  43.6 us (14%)
  between operations  15.2 us (5%)
  local copies, waits for them, and re-layouts  14.8 us (5%)
  other arithmetic  14.6 us (5%)
    all_gather x1, waiting for transfers between devices, body(): lax.all_gather(grad_tok.reshape(rows, student).astype(BF), ('tile', 'segm...  38.5 us
    psum x1, waiting for transfers between devices, body(): folded = lax.psum(dot(embed_z, d_in).astype(BF), 'tile')  29.6 us
    reduce_scatter x1, waiting for transfers between devices, body(): lax.psum_scatter(partial.reshape(S * M, T, share * codes, -1), ('segment'...  28 us
    dot_general x7, matrix products, dot(): return jnp.dot(a, b, preferred_element_type=F32)  21.1 us
    psum x1, waiting for transfers between devices, body(): grad_normed = lax.psum(dot_t(grad_act, enc_in).astype(BF), 'mp').astype(F32)  19.9 us
    dot_general x7, matrix products, dot_t(): lax.dot_general(a, b, (((1,), (1,)), ((), ())), preferred_element_type=F32)  18.5 us
    all_gather x1, waiting for transfers between devices, body(): lax.all_gather(lax.all_gather(grad_own, 'tile'), ('segment', 'mp'))  17.9 us
    reduce_scatter x1, waiting for transfers between devices, body(): own = lax.psum_scatter(own, 'tile', scatter_dimension=0).astype(F32)  17 us
  transfers between devices with their start and end apart: 7, of which 6 were waited for; matrix products, arithmetic and copies ran while one was open for 5% of the time, Pallas kernels for 0%

profile of v1, /device:TPU:0, one launch (start us, length us, event | category | flops | bytes accessed | tf_op | source)
XLA Modules:
  0.0 305.6 jit_solution(12642412171121853214)
XLA Ops:
  7.2 1.4 convolution_convert_fusion.5
  8.8 0.7 fusion.49
  9.6 15.0 %all_gather.29 = bf16[4,16,768]{2,1,0:T(8,128)(2,1)S(1)} all-gather(bf16[1,16,768]{2,1,0:T(8,128)(2,1)S(1)} %all_gather_reshape.3), channel_id=1, replica_groups=mesh['groups'=2,'tile'=4,'segment'=2,'mp'=2] {'tile'}, dimensions={0}, use_global_device_ids=true | all-gather | bytes 122880 | tf_op jit(solution)/shard_map/all_gather | solution.py:67
  25.2 2.2 fusion.50
  27.5 0.7 copy-done.4
  28.2 1.2 convolution_convert_fusion.4
  29.5 13.3 %all-gather.2 = bf16[4,4,2048]{2,1,0:T(4,128)(2,1)S(1)} all-gather(bf16[1,4,2048]{2,1,0:T(4,128)(2,1)S(1)} %bitcast.84), channel_id=1, replica_groups=mesh['groups'=2,'tile'=4,'segment'=2,'mp'=2] {'tile'}, dimensions={0}, use_global_device_ids=true | all-gather | bytes 81920 | tf_op jit(solution)/shard_map/all_gather | solution.py:69
  42.8 2.8 convolution_convert_fusion
  45.7 0.7 convert_element_type.174
  46.3 8.4 %all_gather.31 = bf16[512,672]{0,1:T(8,128)(2,1)S(1)} all-gather(bf16[512,336]{0,1:T(8,128)(2,1)} %param.19), channel_id=1, replica_groups=mesh['groups'=2,'tile'=4,'segment'=2,'mp'=2] {'mp'}, dimensions={1}, use_global_device_ids=true | all-gather | bytes 1032192 | tf_op jit(solution)/shard_map/all_gather | solution.py:70
  54.7 1.0 add_convert_fusion.2
  55.7 0.3 dot_general.61
  56.0 4.2 %multiply_reduce_fusion.1 = (f32[64,16]{1,0:T(8,128)S(1)}, bf16[64,16,2048]{2,1,0:T(8,128)(2,1)}) fusion(f32[16,2048]{1,0:T(8,128)} %convert_element_type.174, bf16[64,16,48]{2,1,0:T(8,128)(2,1)S(1)} %dot_general.61, bf16[48,2048]{1,0:T(8,128)(2,1)} %param.15), kind=kOutput, calls=%fused_computation.7 | convolution fusion | flops 211811328 | bytes 4624384 | tf_op jit(solution)/shard_map/dot_general | solution.py:33
  60.4 29.6 %all-reduce.6.cloned.1.call-done = bf16[64,2048]{1,0:T(8,128)(2,1)} async-done(((bf16[64,2048]{1,0:T(8,128)(2,1)}), bf16[64,2048]{1,0:T(8,128)(2,1)}) %all-reduce.6.cloned.1.call-update) | async-done | bytes 262160 | tf_op jit(solution)/shard_map/psum | solution.py:75
  90.0 0.8 slice_convert_fusion
  90.8 2.2 convolution_add_fusion
  93.0 5.3 %multiply_convert_fusion.1 = bf16[1024,2048]{1,0:T(8,128)(2,1)} fusion(f32[64,16,2048]{2,1,0:T(8,128)S(1)} %convolution_add_fusion, f32[1024]{0:T(1024)S(1)} %rsqrt.37), kind=kLoop, calls=%fused_computation.3 | loop fusion | flops 20971520 | bytes 12587008 | tf_op jit(solution)/shard_map/convert_element_type | solution.py:96
  98.3 7.2 %convolution_convert_fusion.1 = bf16[1024,672]{0,1:T(8,128)(2,1)} fusion(bf16[512,672]{0,1:T(8,128)(2,1)S(1)} %all_gather.31, bf16[1024,2048]{1,0:T(8,128)(2,1)} %multiply_convert_fusion.1, bf16[4096,512]{1,0:T(8,128)(2,1)} %param.18, s32[]{:T(128)S(6)} %select_n.37, bf16[1024,2048]{1,0:T(8,128)(2,1)} %bitcast.86, s32[]{:T(128)S(6)} %select_n.36, ...), kind=kOutput, calls=%fused_computation.22 | convolution fusion | flops 2854912000 | bytes 9404428 | tf_op jit(solution)/shard_map/dot_general | solution.py:33
  105.5 2.6 copy.38
  108.2 28.0 %reduce-scatter.3.cloned.1.call-done = bf16[1,4,64,672]{3,2,1,0:T(8,128)(2,1)} async-done(((bf16[4,4,64,672]{3,2,1,0:T(8,128)(2,1)}), bf16[1,4,64,672]{3,2,1,0:T(8,128)(2,1)}) %reduce-scatter.3.cloned.1.call-update) | async-done | bytes 344080 | tf_op jit(solution)/shard_map/reduce_scatter | solution.py:98
  137.0 1.8 copy.40
  138.8 1.9 reshape.278
  140.7 0.6 convert_reduce_fusion
  142.0 17.0 %reduce-scatter.5.cloned.1.call-done = bf16[1,64,672]{2,1,0:T(8,128)(2,1)} async-done(((bf16[4,64,672]{2,1,0:T(8,128)(2,1)}), bf16[1,64,672]{2,1,0:T(8,128)(2,1)}) %reduce-scatter.5.cloned.1.call-update) | async-done | bytes 86032 | tf_op jit(solution)/shard_map/reduce_scatter | solution.py:101
  159.0 1.0 multiply_convert_fusion.6
  160.0 15.8 %all_gather.32 = bf16[4,64,672]{2,1,0:T(8,128)(2,1)} all-gather(bf16[1,64,672]{2,1,0:T(8,128)(2,1)S(1)} %multiply_convert_fusion.6), channel_id=1, replica_groups=mesh['groups'=2,'tile'=4,'segment'=2,'mp'=2] {'tile'}, dimensions={0}, use_global_device_ids=true | all-gather | bytes 430080 | tf_op jit(solution)/shard_map/all_gather | solution.py:116
  176.1 17.9 %all-gather.9.cloned.1.call-done = bf16[16,64,672]{2,1,0:T(8,128)(2,1)} async-done(((bf16[4,64,672]{2,1,0:T(8,128)(2,1)}), bf16[16,64,672]{2,1,0:T(8,128)(2,1)}) %all-gather.9.cloned.1.call-update) | async-done | bytes 1376272 | tf_op jit(solution)/shard_map/all_gather | solution.py:116
  194.0 2.7 convolution_convert_fusion.2
  196.8 9.2 %multiply_reduce_fusion = (f32[1024]{0:T(1024)S(1)}, bf16[1024,2048]{1,0:T(8,128)(2,1)S(1)}) fusion(f32[64,16,2048]{2,1,0:T(8,128)} %copy-done.1, f32[1024]{0:T(1024)S(1)} %rsqrt.37, bf16[1024,512]{1,0:T(8,128)(2,1)S(1)} %convolution_convert_fusion.2, bf16[4096,512]{1,0:T(8,128)(2,1)S(1)} %copy-done.13, s32[]{:T(128)S(6)} %select_n.37), kind=kOutput, calls=%fused_computation.1 | convolution fusion | flops 2191522816 | bytes 15736836 | tf_op jit(solution)/shard_map/dot_general | solution.py:37
  206.1 0.4 convolution_multiply_fusion.1
  206.5 1.5 fusion.20
  208.0 2.0 fusion.21
  210.0 1.1 copy.41
  211.1 0.9 convert_element_type.197
  212.1 1.0 reshape.280
  213.4 38.5 %all-gather.7.cloned.1.call-done = bf16[16,64,768]{2,1,0:T(8,128)(2,1)} async-done(((bf16[1,64,768]{2,1,0:T(8,128)(2,1)}), bf16[16,64,768]{2,1,0:T(8,128)(2,1)}) %all-gather.7.cloned.1.call-update) | async-done | bytes 1572880 | tf_op jit(solution)/shard_map/all_gather | solution.py:127
  251.9 2.3 reduce_sum.82
  254.2 1.9 fusion.4
  256.1 1.9 fusion.34
  258.0 1.9 fusion.36
  259.9 0.8 convolution_convert_fusion.3
  260.7 0.9 reshape.270
  261.7 0.7 copy.42
  262.5 19.9 %all-reduce.8.cloned.1.call-done = bf16[4,4,4,768]{3,2,0,1:T(4,128)(2,1)} async-done(((bf16[4,4,4,768]{3,2,0,1:T(4,128)(2,1)}), bf16[4,4,4,768]{3,2,0,1:T(4,128)(2,1)}) %all-reduce.8.cloned.1.call-update) | async-done | bytes 98320 | tf_op jit(solution)/shard_map/psum | solution.py:135
  282.5 0.9 multiply_reduce_fusion.4
  283.5 0.7 dynamic-slice_convert_fusion.1
  284.8 13.3 %all-gather.3 = f32[4,224,16]{1,2,0:T(8,128)S(1)} all-gather(f32[1,224,16]{1,2,0:T(8,128)S(1)} %convolution_bitcast_fusion), channel_id=3, replica_groups=mesh['groups'=2,'tile'=4,'segment'=2,'mp'=2] {'tile'}, dimensions={0}, use_global_device_ids=true | all-gather | bytes 71680 | tf_op jit(solution)/shard_map/all_gather | solution.py:143
  298.0 0.7 constant_dynamic-slice_fusion
  (81 shorter events, 3.5 us)
Async XLA Ops:
  7.2 21.0 %copy-start = (bf16[1536,768]{1,0:T(8,128)(2,1)S(1)}, bf16[1536,768]{1,0:T(8,128)(2,1)}, u32[]{:S(2)}) copy-start(bf16[1536,768]{1,0:T(8,128)(2,1)} %param.14) | copy-start | bytes 7077892
  7.2 22.3 %copy-start.11 = (bf16[4,2048]{1,0:T(4,128)(2,1)S(1)}, bf16[4,2048]{1,0:T(4,128)(2,1)}, u32[]{:S(2)}) copy-start(bf16[4,2048]{1,0:T(4,128)(2,1)} %param.16) | copy-start | bytes 49156
  7.2 47.5 %all-reduce.4.cloned.1.call-start = ((), (), s32[]{:S(2)}) async-start(), calls=%async_computation.2 | async-start | bytes 196608 | tf_op jit(solution)/shard_map/psum | solution.py:81
  7.2 35.6 %copy-start.9 = (bf16[48,2048]{1,0:T(8,128)(2,1)S(1)}, bf16[48,2048]{1,0:T(8,128)(2,1)}, u32[]{:S(2)}) copy-start(bf16[48,2048]{1,0:T(8,128)(2,1)} %param.15) | copy-start | bytes 589828
  25.2 4.3 %copy-start.8 = (bf16[64,768]{1,0:T(8,128)(2,1)}, bf16[64,768]{1,0:T(8,128)(2,1)S(1)}, u32[]{:S(2)}) copy-start(bf16[64,768]{1,0:T(8,128)(2,1)S(1)} %multiply_convert_fusion.7) | copy-start | bytes 294916
  27.4 0.8 copy-start.4
  29.4 60.6 %all-reduce.6.cloned.1.call-start = ((), (), s32[]{:S(2)}) async-start(), calls=%async_computation.3 | async-start | bytes 524288 | tf_op jit(solution)/shard_map/psum | solution.py:75
  45.6 90.6 %reduce-scatter.3.cloned.1.call-start = ((), (), s32[]{:S(2)}) async-start(), calls=%async_computation.4 | async-start | bytes 1966080 | tf_op jit(solution)/shard_map/reduce_scatter | solution.py:98
  54.7 43.6 %copy-start.7 = (bf16[512,672]{0,1:T(8,128)(2,1)}, bf16[512,672]{0,1:T(8,128)(2,1)S(1)}, u32[]{:S(2)}) copy-start(bf16[512,672]{0,1:T(8,128)(2,1)S(1)} %all_gather.31) | copy-start | bytes 2064388
  93.0 5.3 %copy-start.1 = (f32[64,16,2048]{2,1,0:T(8,128)}, f32[64,16,2048]{2,1,0:T(8,128)S(1)}, u32[]{:S(2)}) copy-start(f32[64,16,2048]{2,1,0:T(8,128)S(1)} %convolution_add_fusion) | copy-start | bytes 25165828
  105.5 30.8 %copy-start.12 = (s32[2,32]{1,0:T(2,128)S(1)}, s32[2,32]{1,0:T(2,128)}, u32[]{:S(2)}) copy-start(s32[2,32]{1,0:T(2,128)} %param.11) | copy-start | bytes 772
  105.5 31.2 %copy-start.3 = (bf16[2,8,48,224]{3,2,1,0:T(8,128)(2,1)S(1)}, bf16[2,8,48,224]{3,2,1,0:T(8,128)(2,1)}, u32[]{:S(2)}) copy-start(bf16[2,8,48,224]{3,2,1,0:T(8,128)(2,1)} %param.10) | copy-start | bytes 1032196
  108.2 50.8 %reduce-scatter.5.cloned.1.call-start = ((), (), s32[]{:S(2)}) async-start(), calls=%async_computation.5 | async-start | bytes 491520 | tf_op jit(solution)/shard_map/reduce_scatter | solution.py:101
  136.3 57.7 %all-gather.9.cloned.1.call-start = ((), (), s32[]{:S(2)}) async-start(), calls=%async_computation.8 | async-start | bytes 1966080 | tf_op jit(solution)/shard_map/all_gather | solution.py:116
  175.8 76.1 %all-gather.7.cloned.1.call-start = ((), (), s32[]{:S(2)}) async-start(), calls=%async_computation.6 | async-start | bytes 1671168 | tf_op jit(solution)/shard_map/all_gather | solution.py:127
  194.0 2.9 copy-start.13
  196.8 9.2 %copy-start.10 = (bf16[48,2048]{1,0:T(8,128)(2,1)S(1)}, bf16[48,2048]{1,0:T(8,128)(2,1)}, u32[]{:S(2)}) copy-start(bf16[48,2048]{1,0:T(8,128)(2,1)} %param.15) | copy-start | bytes 589828
  196.8 9.7 %copy-start.14 = (bf16[64,16,2048]{2,1,0:T(8,128)(2,1)S(1)}, bf16[64,16,2048]{2,1,0:T(8,128)(2,1)}, u32[]{:S(2)}) copy-start(bf16[64,16,2048]{2,1,0:T(8,128)(2,1)} %get-tuple-element.6) | copy-start | bytes 12582916
  206.5 1.5 copy-start.6
  208.0 46.2 %copy-start.5 = (f32[64,1536]{1,0:T(8,128)S(1)}, f32[64,1536]{1,0:T(8,128)}, u32[]{:S(2)}) copy-start(f32[64,1536]{1,0:T(8,128)} %copy-done.4) | copy-start | bytes 1179652
  212.0 70.5 %all-reduce.8.cloned.1.call-start = ((), (), s32[]{:S(2)}) async-start(), calls=%async_computation.7 | async-start | bytes 196608 | tf_op jit(solution)/shard_map/psum | solution.py:135
  254.2 5.7 %copy-start.2 = (bf16[768,1536]{1,0:T(8,128)(2,1)S(1)}, bf16[768,1536]{1,0:T(8,128)(2,1)}, u32[]{:S(2)}) copy-start(bf16[768,1536]{1,0:T(8,128)(2,1)} %param.13) | copy-start | bytes 7077892
Sparse Core Ops, SparseCore 0:
  29.5 22.1 all-reduce.3
  54.6 35.3 all-reduce.5
  108.3 27.9 reduce-scatter.2
  138.4 20.5 reduce-scatter.4
  176.0 17.9 all-gather.8
  212.2 39.7 all-gather.6
  262.5 19.9 all-reduce.7
